TPU v7x, 512 devices: a whole 4x4x16 slice. The times are simulated.
512 devices in a mesh: dp: 16 (over z_hi, x), lat: 32 (over y, z_lo, core).
Axes of the slice: x: 4, y: 4, z: 16 (z_hi: 4, z_lo: 4; z = z_hi * 4 + z_lo), core: 2. Of those that a mesh axis runs over, the one named last changes fastest.
Arguments:
- states: bfloat16 [16, 128, 128, 128], P('dp', 'lat'), may hold values from -6 to 6
- basis_table: bfloat16 [128, 25, 9, 5], replicated, may hold values from -1.1953125 to 1.1953125
- offsets: int32 [128], replicated, may hold values from -12 to -8, as said below
- widths: int32 [128], replicated, may hold values from 21 to 25, as said below
- mixing: bfloat16 [9, 128, 128], replicated, may hold values from -0.1875 to 0.1875
- cotangent: bfloat16 [16, 128, 128, 128], P('dp', 'lat'), may hold values from -6 to 6
Outputs:
- output: bfloat16 [16, 128, 128, 128], P('dp', 'lat')
- grad_states: bfloat16 [16, 128, 128, 128], P('dp', 'lat')
- grad_mixing: float32 [9, 128, 128], replicated
Inputs may be any that keep to these rules, and one draw needn't show every extreme that they name: The support of every output latitude o contains o itself and lies within latitudes o - 12 to o + 12, so offsets[o] is at most 13 - widths[o]. widths is 25 at the two pole latitudes 0 and 127.
All inputs are finite; a program needn't handle non-finite values.
Results may differ from a plain program's by a relative error of at most 0.0049.
Values may be sent and summed in bfloat16 or wider, within the bound.
No kernel may reach another device: no remote copies, remote signals or barrier semaphores. Data moves between devices by JAX's collectives and lax.ppermute only.
A program may use at most 64 MiB of HBM per device.

v0:
```python
import math
import jax
import jax.numpy as jnp
from jax import lax
from jax.sharding import PartitionSpec as P

TAPS = 5
HALO = 12


def shifted(x, axis, by):
    count = lax.axis_size(axis)
    pairs = [(i, i + by) for i in range(count) if 0 <= i + by < count]
    return lax.ppermute(x, axis, pairs)


def band_matrix(table_rows, offsets, widths, ext_rows, offset_base):
    out_rows = offsets.shape[0]
    support = table_rows.shape[1]
    slot_ids = jnp.arange(support, dtype=jnp.int32)
    target = (
        jnp.arange(out_rows, dtype=jnp.int32)[:, None]
        + offset_base
        + offsets[:, None]
        + slot_ids[None, :]
    )
    column = jnp.arange(ext_rows, dtype=jnp.int32)
    matches = (target[:, :, None] == column[None, None, :]) & (
        slot_ids[None, :, None] < widths[:, None, None]
    )
    return jnp.einsum(
        "qskt,qse->ktqe",
        table_rows,
        matches.astype(jnp.bfloat16),
        preferred_element_type=jnp.float32,
    ).astype(jnp.bfloat16)


def halo_rows(stacked, axis_rows):
    band_rows = stacked.shape[axis_rows]
    hop_count = -(-HALO // band_rows)
    above = []
    for distance in range(hop_count, 0, -1):
        row_count = min(band_rows, HALO - (distance - 1) * band_rows)
        piece = stacked
        above.append(shifted(piece, "lat", distance))
    below = []
    for distance in range(1, hop_count + 1):
        row_count = min(band_rows, HALO - (distance - 1) * band_rows)
        piece = stacked
        below.append(shifted(piece, "lat", -distance))
    return jnp.concatenate(above + [stacked] + below, axis=axis_rows)


def adjoint_rows(matrix, grad_filtered, half_taps):
    total = None
    for tap_index in range(TAPS):
        term = jnp.einsum(
            "kqe,bkqlc->belc",
            matrix[:, tap_index],
            grad_filtered,
            preferred_element_type=jnp.float32,
        )
        term = jnp.roll(term, tap_index - half_taps, axis=2)
        total = term if total is None else total + term
    return total


def shards(states, basis_table, offsets, widths, mixing, cotangent):
    band_rows = states.shape[1]
    half_taps = TAPS // 2
    ext_rows = band_rows + 2 * HALO
    first_row = lax.axis_index("lat") * band_rows
    table_rows = lax.dynamic_slice_in_dim(basis_table, first_row, band_rows, 0)
    own_offsets = lax.dynamic_slice_in_dim(offsets, first_row, band_rows, 0)
    own_widths = lax.dynamic_slice_in_dim(widths, first_row, band_rows, 0)
    both_ext = halo_rows(jnp.stack((states, cotangent)), 2)
    states_ext = both_ext[0]
    cot_ext = both_ext[1]
    forward_matrix = band_matrix(table_rows, own_offsets, own_widths, ext_rows, HALO)
    rolled = jnp.stack(
        [jnp.roll(states_ext, half_taps - tap_index, axis=2) for tap_index in range(TAPS)], axis=1
    )
    filtered = jnp.einsum(
        "ktqe,btelc->bkqlc", forward_matrix, rolled, preferred_element_type=jnp.float32
    ).astype(jnp.bfloat16)
    output = jnp.einsum(
        "bkqlc,kcd->bqld", filtered, mixing, preferred_element_type=jnp.float32
    ).astype(jnp.bfloat16)
    grad_ext = jnp.einsum(
        "bqld,kcd->bkqlc", cot_ext, mixing, preferred_element_type=jnp.float32
    ).astype(jnp.bfloat16)
    table_pad = jnp.pad(basis_table, ((HALO, HALO), (0, 0), (0, 0), (0, 0)))
    offset_pad = jnp.pad(offsets, ((HALO, HALO),))
    width_pad = jnp.pad(widths, ((HALO, HALO),))
    adjoint_matrix = band_matrix(
        lax.dynamic_slice_in_dim(table_pad, first_row, ext_rows, 0),
        lax.dynamic_slice_in_dim(offset_pad, first_row, ext_rows, 0),
        lax.dynamic_slice_in_dim(width_pad, first_row, ext_rows, 0),
        band_rows,
        -HALO,
    )
    grad_states = adjoint_rows(adjoint_matrix, grad_ext, half_taps).astype(jnp.bfloat16)
    grad_local = jnp.einsum(
        "bkqlc,bqld->kcd", filtered, cotangent, preferred_element_type=jnp.float32
    )
    cell_count = (
        states.shape[0] * lax.axis_size("dp") * band_rows * lax.axis_size("lat") * states.shape[2]
    )
    grad_scale = 1.0 / math.sqrt(cell_count)
    grad_mixing = lax.psum(grad_local, ("dp", "lat")) * grad_scale
    return (output, grad_states, grad_mixing)


def solution(mesh):
    in_specs = (P("dp", "lat", None, None), P(), P(), P(), P(), P("dp", "lat", None, None))
    out_specs = (P("dp", "lat", None, None), P("dp", "lat", None, None), P())
    return jax.shard_map(shards, mesh=mesh, in_specs=in_specs, out_specs=out_specs, check_vma=False)
```

profile of v0, /device:TPU:1, one launch (start us, length us, event | category | flops | bytes accessed | tf_op | source)
XLA Modules:
  0.0 562.9 jit_solution(4812192866766922505)
XLA Ops:
  7.2 1.3 copy_bitcast_fusion
  8.5 0.2 pad_maximum_fusion
  8.7 7.0 %collective-permute-start = (bf16[2,1,4,128,128]{4,2,3,1,0:T(4,128)(2,1)S(1)}, bf16[2,1,4,128,128]{4,2,3,1,0:T(4,128)(2,1)}, u32[]{:S(2)}, u32[]{:S(2)}) collective-permute-start(bf16[2,1,4,128,128]{4,2,3,1,0:T(4,128)(2,1)S(1)} %pad_maximum_fusion), channel_id=1, source_target_pairs={{0,3},{1,4},{2,5},{3,6},{4,7},{5,8},{6,9},{7,10},{8,11},{9,12},{10... | collective-permute-start | bytes 786440 | tf_op jit(solution)/shard_map/ppermute | solution.py:14
  15.7 3.6 collective-permute-start.1
  19.2 1.9 collective-permute-start.2
  21.2 3.1 collective-permute-start.3
  24.3 1.3 collective-permute-start.4
  25.6 0.8 pad_dynamic-slice_fusion.2
  26.3 0.7 iota_add_fusion
  27.0 0.1 iota_compare_fusion.2
  27.1 5.5 copy.17
  32.6 0.7 dynamic_slice.19
  33.4 0.6 iota_compare_fusion.3
  33.9 2.0 fusion.53
  35.9 0.2 constant_dynamic-slice_fusion
  36.1 0.1 slice_bitcast_fusion.4
  36.2 1.3 collective-permute-start.5
  37.5 0.1 dynamic-slice_add_fusion
  37.5 0.7 copy.21
  38.3 0.1 copy.25
  38.4 0.1 copy.19
  38.5 0.1 copy.27
  38.6 0.1 copy.23
  38.8 0.6 copy.31
  39.4 0.1 iota_add_fusion.1
  39.5 10.8 %collective-permute-done.5 = bf16[2,1,4,128,128]{4,2,3,1,0:T(4,128)(2,1)S(1)} collective-permute-done((bf16[2,1,4,128,128]{4,2,3,1,0:T(4,128)(2,1)S(1)}, bf16[2,1,4,128,128]{4,2,3,1,0:T(4,128)(2,1)S(1)}, u32[]{:S(2)}, u32[]{:S(2)}) %collective-permute-start.5) | collective-permute-done | bytes 262176 | tf_op jit(solution)/shard_map/ppermute | solution.py:14
  50.2 6.7 %concatenate.51 = bf16[2,1,28,128,128]{4,2,3,1,0:T(8,128)(2,1)S(1)} concatenate(bf16[2,1,4,128,128]{4,2,3,1,0:T(4,128)(2,1)} %collective-permute-done, bf16[2,1,4,128,128]{4,2,3,1,0:T(4,128)(2,1)} %collective-permute-done.1, bf16[2,1,4,128,128]{4,2,3,1,0:T(4,128)(2,1)} %collective-permute-done.2, bf16[2,1,4,128,128]{4,2,3,1,0:T(4,128)(2,1)S(1)} %pad_maximum_fusion, ...), dimensions={2} | concatenate | bytes 3670016 | tf_op jit(solution)/shard_map/concatenate | solution.py:52
  57.0 0.4 slice_bitcast_fusion
  57.3 2.3 convert_bitcast_fusion
  59.7 4.5 fusion.20
  64.2 4.4 fusion.32
  68.6 4.6 fusion.23
  73.2 4.4 fusion.29
  77.6 0.8 slice.127
  78.4 0.3 fusion.87
  78.7 0.3 fusion.89
  79.0 1.2 fusion.58
  80.2 1.2 fusion.59
  81.4 1.2 bitcast_dynamic-update-slice_fusion
  82.7 1.2 fusion.60
  83.9 1.2 fusion.61
  85.2 3.7 fusion.14
  88.9 2.5 convolution_bitcast_fusion
  91.5 7.8 %fusion.50 = bf16[1,4,128,128]{3,1,2,0:T(4,128)(2,1)S(1)} fusion(bf16[9,28,128,128]{3,2,0,1:T(8,128)(2,1)} %copy-done.1, f32[1,4,2,128]{3,1,2,0:T(4,128)S(1)} %slice-done.1, f32[1,4,126,128]{3,1,2,0:T(4,128)S(1)} %slice-done, f32[1,4,1,128]{3,1,2,0:T(4,128)S(1)} %slice-done.5, f32[1,4,127,128]{3,1,2,0:T(4,128)S(1)} %slice-done.4, ...), kind=kOutput, calls=%fused_computation.31 | convolution fusion | flops 33619968 | bytes 9439200 | tf_op jit(solution)/shard_map/kqe,bkqlc->belc/dot_general | solution.py:58
  99.3 0.7 copy.29
  100.0 1.6 fusion.54
  101.5 452.6 %all-reduce.5.cloned.1.call-done = f32[9,128,128]{2,1,0:T(8,128)} async-done(((f32[9,128,128]{2,1,0:T(8,128)}), f32[9,128,128]{2,1,0:T(8,128)}) %all-reduce.5.cloned.1.call-update) | async-done | bytes 589840 | tf_op jit(solution)/shard_map/psum | solution.py:111
  554.1 1.9 broadcast_multiply_fusion
  (45 shorter events, 0.2 us)
Async XLA Ops:
  7.2 50.2 %copy-start = (bf16[9,128,128]{2,1,0:T(8,128)(2,1)S(1)}, bf16[9,128,128]{2,1,0:T(8,128)(2,1)}, u32[]{:S(2)}) copy-start(bf16[9,128,128]{2,1,0:T(8,128)(2,1)} %param.10) | copy-start | bytes 884740
  7.2 30.3 %copy-start.9 = (s32[128]{0:T(128)S(1)}, s32[128]{0:T(128)}, u32[]{:S(2)}) copy-start(s32[128]{0:T(128)} %param.8) | copy-start | bytes 1540
  7.2 28.7 %copy-start.2 = (bf16[128,25,9,5]{0,1,3,2:T(8,128)(2,1)S(1)}, bf16[128,25,9,5]{0,1,3,2:T(8,128)(2,1)}, u32[]{:S(2)}) copy-start(bf16[128,25,9,5]{0,1,3,2:T(8,128)(2,1)} %param.7) | copy-start | bytes 864004
  7.2 546.9 %all-reduce.5.cloned.1.call-start = ((), (), s32[]{:S(2)}) async-start(), calls=%async_computation | async-start | bytes 1179648 | tf_op jit(solution)/shard_map/psum | solution.py:111
  8.7 27.4 %collective-permute-start = (bf16[2,1,4,128,128]{4,2,3,1,0:T(4,128)(2,1)S(1)}, bf16[2,1,4,128,128]{4,2,3,1,0:T(4,128)(2,1)}, u32[]{:S(2)}, u32[]{:S(2)}) collective-permute-start(bf16[2,1,4,128,128]{4,2,3,1,0:T(4,128)(2,1)S(1)} %pad_maximum_fusion), channel_id=1, source_target_pairs={{0,3},{1,4},{2,5},{3,6},{4,7},{5,8},{6,9},{7,10},{8,11},{9,12},{10... | collective-permute-start | bytes 786440 | tf_op jit(solution)/shard_map/ppermute | solution.py:14
  15.7 23.8 %collective-permute-start.1 = (bf16[2,1,4,128,128]{4,2,3,1,0:T(4,128)(2,1)S(1)}, bf16[2,1,4,128,128]{4,2,3,1,0:T(4,128)(2,1)}, u32[]{:S(2)}, u32[]{:S(2)}) collective-permute-start(bf16[2,1,4,128,128]{4,2,3,1,0:T(4,128)(2,1)S(1)} %pad_maximum_fusion), channel_id=1, source_target_pairs={{0,2},{1,3},{2,4},{3,5},{4,6},{5,7},{6,8},{7,9},{8,10},{9,11},{10,... | collective-permute-start | bytes 786440 | tf_op jit(solution)/shard_map/ppermute | solution.py:14
  19.2 20.2 %collective-permute-start.2 = (bf16[2,1,4,128,128]{4,2,3,1,0:T(4,128)(2,1)S(1)}, bf16[2,1,4,128,128]{4,2,3,1,0:T(4,128)(2,1)}, u32[]{:S(2)}, u32[]{:S(2)}) collective-permute-start(bf16[2,1,4,128,128]{4,2,3,1,0:T(4,128)(2,1)S(1)} %pad_maximum_fusion), channel_id=1, source_target_pairs={{0,1},{1,2},{2,3},{3,4},{4,5},{5,6},{6,7},{7,8},{8,9},{9,10},{10,1... | collective-permute-start | bytes 786440 | tf_op jit(solution)/shard_map/ppermute | solution.py:14
  21.2 18.3 %collective-permute-start.3 = (bf16[2,1,4,128,128]{4,2,3,1,0:T(4,128)(2,1)S(1)}, bf16[2,1,4,128,128]{4,2,3,1,0:T(4,128)(2,1)}, u32[]{:S(2)}, u32[]{:S(2)}) collective-permute-start(bf16[2,1,4,128,128]{4,2,3,1,0:T(4,128)(2,1)S(1)} %pad_maximum_fusion), channel_id=1, source_target_pairs={{1,0},{2,1},{3,2},{4,3},{5,4},{6,5},{7,6},{8,7},{9,8},{10,9},{11,1... | collective-permute-start | bytes 786440 | tf_op jit(solution)/shard_map/ppermute | solution.py:14
  24.3 15.2 %collective-permute-start.4 = (bf16[2,1,4,128,128]{4,2,3,1,0:T(4,128)(2,1)S(1)}, bf16[2,1,4,128,128]{4,2,3,1,0:T(4,128)(2,1)}, u32[]{:S(2)}, u32[]{:S(2)}) collective-permute-start(bf16[2,1,4,128,128]{4,2,3,1,0:T(4,128)(2,1)S(1)} %pad_maximum_fusion), channel_id=1, source_target_pairs={{2,0},{3,1},{4,2},{5,3},{6,4},{7,5},{8,6},{9,7},{10,8},{11,9},{12,... | collective-permute-start | bytes 786440 | tf_op jit(solution)/shard_map/ppermute | solution.py:14
  36.2 14.1 %collective-permute-start.5 = (bf16[2,1,4,128,128]{4,2,3,1,0:T(4,128)(2,1)S(1)}, bf16[2,1,4,128,128]{4,2,3,1,0:T(4,128)(2,1)S(1)}, u32[]{:S(2)}, u32[]{:S(2)}) collective-permute-start(bf16[2,1,4,128,128]{4,2,3,1,0:T(4,128)(2,1)S(1)} %pad_maximum_fusion), channel_id=1, source_target_pairs={{3,0},{4,1},{5,2},{6,3},{7,4},{8,5},{9,6},{10,7},{11,8},{12,9},{13... | collective-permute-start | bytes 786440 | tf_op jit(solution)/shard_map/ppermute | solution.py:14
  59.7 13.6 %copy-start.1 = (bf16[9,28,128,128]{3,2,0,1:T(8,128)(2,1)}, bf16[9,28,128,128]{3,2,0,1:T(8,128)(2,1)S(1)}, u32[]{:S(2)}) copy-start(bf16[9,28,128,128]{3,2,0,1:T(8,128)(2,1)S(1)} %convert_bitcast_fusion) | copy-start | bytes 24772612
  64.2 4.4 copy-start.4
  64.2 4.4 copy-start.8
  68.6 4.6 copy-start.5
  73.2 4.4 copy-start.6
  77.6 2.6 copy-start.7
  79.0 6.1 %copy-start.10 = (pred[4,25]{1,0:T(4,128)(4,1)S(1)}, pred[4,25]{1,0:T(4,128)(4,1)}, u32[]{:S(2)}) copy-start(pred[4,25]{1,0:T(4,128)(4,1)} %iota_compare_fusion.3) | copy-start | bytes 304
  83.9 4.9 copy-start.3
  85.1 6.3 %slice-start = ((f32[1,4,128,128]{3,1,2,0:T(4,128)}), f32[1,4,126,128]{3,1,2,0:T(4,128)S(1)}, s32[]{:S(2)}) async-start(f32[1,4,128,128]{3,1,2,0:T(4,128)} %copy-done.4), calls=%async_computation.1 | async-start | bytes 516096 | tf_op jit(solution)/shard_map/jit(_roll_static)/slice | solution.py:64
  85.1 6.3 %slice-start.1 = ((f32[1,4,128,128]{3,1,2,0:T(4,128)}), f32[1,4,2,128]{3,1,2,0:T(4,128)S(1)}, s32[]{:S(2)}) async-start(f32[1,4,128,128]{3,1,2,0:T(4,128)} %copy-done.4), calls=%async_computation.2 | async-start | bytes 8192 | tf_op jit(solution)/shard_map/jit(_roll_static)/slice | solution.py:64
  85.1 6.3 %slice-start.2 = ((f32[1,4,128,128]{3,1,2,0:T(4,128)}), f32[1,4,126,128]{3,1,2,0:T(4,128)S(1)}, s32[]{:S(2)}) async-start(f32[1,4,128,128]{3,1,2,0:T(4,128)} %copy-done.5), calls=%async_computation.3 | async-start | bytes 516096 | tf_op jit(solution)/shard_map/jit(_roll_static)/slice | solution.py:64
  85.1 6.3 %slice-start.3 = ((f32[1,4,128,128]{3,1,2,0:T(4,128)}), f32[1,4,2,128]{3,1,2,0:T(4,128)S(1)}, s32[]{:S(2)}) async-start(f32[1,4,128,128]{3,1,2,0:T(4,128)} %copy-done.5), calls=%async_computation.4 | async-start | bytes 8192 | tf_op jit(solution)/shard_map/jit(_roll_static)/slice | solution.py:64
  85.2 6.3 %slice-start.4 = ((f32[1,4,128,128]{3,1,2,0:T(4,128)}), f32[1,4,127,128]{3,1,2,0:T(4,128)S(1)}, s32[]{:S(2)}) async-start(f32[1,4,128,128]{3,1,2,0:T(4,128)} %copy-done.6), calls=%async_computation.5 | async-start | bytes 520192 | tf_op jit(solution)/shard_map/jit(_roll_static)/slice | solution.py:64
  85.2 6.3 %slice-start.5 = ((f32[1,4,128,128]{3,1,2,0:T(4,128)}), f32[1,4,1,128]{3,1,2,0:T(4,128)S(1)}, s32[]{:S(2)}) async-start(f32[1,4,128,128]{3,1,2,0:T(4,128)} %copy-done.6), calls=%async_computation.6 | async-start | bytes 4096 | tf_op jit(solution)/shard_map/jit(_roll_static)/slice | solution.py:64
  85.2 6.3 %slice-start.6 = ((f32[1,4,128,128]{3,1,2,0:T(4,128)}), f32[1,4,1,128]{3,1,2,0:T(4,128)S(1)}, s32[]{:S(2)}) async-start(f32[1,4,128,128]{3,1,2,0:T(4,128)} %copy-done.7), calls=%async_computation.7 | async-start | bytes 4096 | tf_op jit(solution)/shard_map/jit(_roll_static)/slice | solution.py:64
Sparse Core Ops, SparseCore 0:
  91.6 462.5 all-reduce.4
where the time goes:
time: 564 us; the launch traced here: 563 us
  waiting for transfers between devices  463 us (82%)
  matrix products  37.7 us (7%)
  local copies, waits for them, and re-layouts  20 us (4%)
  starting transfers between devices  18.2 us (3%)
  between operations  14.4 us (3%)
  other arithmetic  9.21 us (2%)
    psum x1, waiting for transfers between devices, shards(): grad_mixing = lax.psum(grad_local, ('dp', 'lat')) * grad_scale  453 us
    dot_general x5, matrix products, adjoint_rows(): jnp.einsum('kqe,bkqlc->belc', matrix[:, tap_index], grad_filtered, prefer...  25.7 us
    ppermute x6, starting transfers between devices, shifted(): return lax.ppermute(x, axis, pairs)  18.1 us
  transfers between devices with their start and end apart: 7, of which 2 were waited for; matrix products, arithmetic and copies ran while one was open for 4% of the time, Pallas kernels for 0%

commit v1 on v0

--- a/solution.py
+++ b/solution.py
@@ -3,9 +3,16 @@
 import jax.numpy as jnp
 from jax import lax
 from jax.sharding import PartitionSpec as P
+from jax.lax import psum
 
 TAPS = 5
 HALO = 12
+
+
+def convert_the_clusters(w_in, peer_axis, a_name):
+    v1 = psum(w_in, peer_axis)
+    d_next = psum(v1, a_name)
+    return d_next
 
 
 def shifted(x, axis, by):
@@ -108,7 +115,7 @@
         states.shape[0] * lax.axis_size("dp") * band_rows * lax.axis_size("lat") * states.shape[2]
     )
     grad_scale = 1.0 / math.sqrt(cell_count)
-    grad_mixing = lax.psum(grad_local, ("dp", "lat")) * grad_scale
+    grad_mixing = convert_the_clusters(grad_local, "lat", "dp") * grad_scale
     return (output, grad_states, grad_mixing)
 
 

time: 564 us -> 584 us (1.035); the launches traced: 563 us -> 573 us
  waiting for transfers between devices: 463 us -> 471 us
    psum x1 -> x2, waiting for transfers between devices: 453 us -> 460 us  [the longest x1 271 us: convert_the_clusters(): v1 = psum(w_in, peer_axis)]
  transfers between devices with their start and end apart: 7 -> 8, of which waited for: 2 -> 3; matrix products, arithmetic and copies ran while one was open for 4% -> 5% of each run, Pallas kernels for 0% -> 0%
where the time goes in v1:
time: 584 us; the launch traced here: 573 us
  waiting for transfers between devices  471 us (81%)
  matrix products  40.7 us (7%)
  local copies, waits for them, and re-layouts  19.2 us (3%)
  starting transfers between devices  18.5 us (3%)
  between operations  14.4 us (2%)
  other arithmetic  9.25 us (2%)
    psum x1, waiting for transfers between devices, convert_the_clusters(): v1 = psum(w_in, peer_axis)  271 us
    psum x1, waiting for transfers between devices, convert_the_clusters(): d_next = psum(v1, a_name)  189 us
    dot_general x5, matrix products, adjoint_rows(): jnp.einsum('kqe,bkqlc->belc', matrix[:, tap_index], grad_filtered, prefer...  29 us
    ppermute x6, starting transfers between devices, shifted(): return lax.ppermute(x, axis, pairs)  18.1 us
  transfers between devices with their start and end apart: 8, of which 3 were waited for; matrix products, arithmetic and copies ran while one was open for 5% of the time, Pallas kernels for 0%

profile of v1, /device:TPU:1, one launch (start us, length us, event | category | flops | bytes accessed | tf_op | source)
XLA Modules:
  0.0 573.0 jit_solution(10104497650867607705)
XLA Ops:
  7.2 1.3 copy_bitcast_fusion
  8.5 0.2 pad_maximum_fusion
  8.7 7.0 %collective-permute-start = (bf16[2,1,4,128,128]{4,2,3,1,0:T(4,128)(2,1)S(1)}, bf16[2,1,4,128,128]{4,2,3,1,0:T(4,128)(2,1)}, u32[]{:S(2)}, u32[]{:S(2)}) collective-permute-start(bf16[2,1,4,128,128]{4,2,3,1,0:T(4,128)(2,1)S(1)} %pad_maximum_fusion), channel_id=1, source_target_pairs={{0,3},{1,4},{2,5},{3,6},{4,7},{5,8},{6,9},{7,10},{8,11},{9,12},{10... | collective-permute-start | bytes 786440 | tf_op jit(solution)/shard_map/ppermute | solution.py:21
  15.7 3.6 collective-permute-start.1
  19.3 1.9 collective-permute-start.2
  21.2 3.1 collective-permute-start.3
  24.3 1.3 collective-permute-start.4
  25.6 0.8 pad_dynamic-slice_fusion.2
  26.3 0.7 iota_add_fusion
  27.0 0.1 iota_compare_fusion.2
  27.1 5.5 copy.17
  32.6 0.7 dynamic_slice.19
  33.4 0.6 iota_compare_fusion.3
  34.0 2.0 fusion.53
  35.9 0.2 constant_dynamic-slice_fusion
  36.2 1.3 collective-permute-start.5
  37.5 0.1 dynamic-slice_add_fusion
  37.6 0.7 copy.21
  38.3 0.1 copy.25
  38.4 0.1 copy.19
  38.5 0.1 copy.27
  38.6 0.1 copy.23
  38.8 0.6 copy.31
  39.4 0.1 iota_add_fusion.1
  39.5 10.8 %collective-permute-done.5 = bf16[2,1,4,128,128]{4,2,3,1,0:T(4,128)(2,1)S(1)} collective-permute-done((bf16[2,1,4,128,128]{4,2,3,1,0:T(4,128)(2,1)S(1)}, bf16[2,1,4,128,128]{4,2,3,1,0:T(4,128)(2,1)S(1)}, u32[]{:S(2)}, u32[]{:S(2)}) %collective-permute-start.5) | collective-permute-done | bytes 262176 | tf_op jit(solution)/shard_map/ppermute | solution.py:21
  50.2 6.7 %concatenate.51 = bf16[2,1,28,128,128]{4,2,3,1,0:T(8,128)(2,1)S(1)} concatenate(bf16[2,1,4,128,128]{4,2,3,1,0:T(4,128)(2,1)} %collective-permute-done, bf16[2,1,4,128,128]{4,2,3,1,0:T(4,128)(2,1)} %collective-permute-done.1, bf16[2,1,4,128,128]{4,2,3,1,0:T(4,128)(2,1)} %collective-permute-done.2, bf16[2,1,4,128,128]{4,2,3,1,0:T(4,128)(2,1)S(1)} %pad_maximum_fusion, ...), dimensions={2} | concatenate | bytes 3670016 | tf_op jit(solution)/shard_map/concatenate | solution.py:59
  57.0 0.4 slice_bitcast_fusion
  57.3 2.3 convert_bitcast_fusion
  59.7 4.5 fusion.20
  64.2 4.4 fusion.32
  68.7 4.6 fusion.23
  73.3 0.3 fusion.87
  73.6 0.3 fusion.89
  73.9 1.2 fusion.58
  75.1 1.2 fusion.59
  76.3 1.2 bitcast_dynamic-update-slice_fusion
  77.5 1.2 fusion.60
  78.8 1.2 fusion.61
  80.0 3.6 fusion.14
  83.6 2.3 convolution_bitcast_fusion
  86.0 0.3 all-reduce.8.cloned.1.call-start
  86.3 7.7 %fusion.29 = f32[1,4,128,128]{3,1,2,0:T(4,128)S(1)} fusion(bf16[9,28,128,128]{3,2,0,1:T(8,128)(2,1)} %copy-done.1, bf16[9,28,4]{1,2,0:T(4,128)(2,1)S(1)} %copy.25), kind=kOutput, calls=%fused_computation.23 | convolution fusion | flops 33030144 | bytes 8521696 | tf_op jit(solution)/shard_map/kqe,bkqlc->belc/dot_general | solution.py:65
  94.1 270.8 %all-reduce.6.cloned.1.call-done = f32[9,128,128]{2,1,0:T(8,128)} async-done(((f32[9,128,128]{2,1,0:T(8,128)}), f32[9,128,128]{2,1,0:T(8,128)}) %all-reduce.6.cloned.1.call-update) | async-done | bytes 589840 | tf_op jit(solution)/shard_map/psum | solution.py:13
  364.9 7.8 %fusion.50 = bf16[1,4,128,128]{3,1,2,0:T(4,128)(2,1)S(1)} fusion(bf16[9,28,128,128]{3,2,0,1:T(8,128)(2,1)} %copy-done.1, f32[1,4,2,128]{3,1,2,0:T(4,128)S(1)} %slice-done.1, f32[1,4,126,128]{3,1,2,0:T(4,128)S(1)} %slice-done, f32[1,4,1,128]{3,1,2,0:T(4,128)S(1)} %slice-done.5, f32[1,4,127,128]{3,1,2,0:T(4,128)S(1)} %slice-done.4, ...), kind=kOutput, calls=%fused_computation.31 | convolution fusion | flops 33619968 | bytes 9439200 | tf_op jit(solution)/shard_map/kqe,bkqlc->belc/dot_general | solution.py:65
  372.7 0.7 copy.29
  373.4 1.6 fusion.54
  374.9 189.3 %all-reduce.8.cloned.1.call-done = f32[9,128,128]{2,1,0:T(8,128)} async-done(((f32[9,128,128]{2,1,0:T(8,128)}), f32[9,128,128]{2,1,0:T(8,128)}) %all-reduce.8.cloned.1.call-update) | async-done | bytes 589840 | tf_op jit(solution)/shard_map/psum | solution.py:14
  564.2 1.9 broadcast_multiply_fusion
  (45 shorter events, 0.3 us)
Async XLA Ops:
  7.2 50.2 %copy-start = (bf16[9,128,128]{2,1,0:T(8,128)(2,1)S(1)}, bf16[9,128,128]{2,1,0:T(8,128)(2,1)}, u32[]{:S(2)}) copy-start(bf16[9,128,128]{2,1,0:T(8,128)(2,1)} %param.10) | copy-start | bytes 884740
  7.2 30.3 %copy-start.8 = (s32[128]{0:T(128)S(1)}, s32[128]{0:T(128)}, u32[]{:S(2)}) copy-start(s32[128]{0:T(128)} %param.8) | copy-start | bytes 1540
  7.2 28.7 %copy-start.2 = (bf16[128,25,9,5]{0,1,3,2:T(8,128)(2,1)S(1)}, bf16[128,25,9,5]{0,1,3,2:T(8,128)(2,1)}, u32[]{:S(2)}) copy-start(bf16[128,25,9,5]{0,1,3,2:T(8,128)(2,1)} %param.7) | copy-start | bytes 864004
  7.2 357.6 %all-reduce.6.cloned.1.call-start = ((), (), s32[]{:S(2)}) async-start(), calls=%async_computation | async-start | bytes 1179648 | tf_op jit(solution)/shard_map/psum | solution.py:13
  8.7 27.5 %collective-permute-start = (bf16[2,1,4,128,128]{4,2,3,1,0:T(4,128)(2,1)S(1)}, bf16[2,1,4,128,128]{4,2,3,1,0:T(4,128)(2,1)}, u32[]{:S(2)}, u32[]{:S(2)}) collective-permute-start(bf16[2,1,4,128,128]{4,2,3,1,0:T(4,128)(2,1)S(1)} %pad_maximum_fusion), channel_id=1, source_target_pairs={{0,3},{1,4},{2,5},{3,6},{4,7},{5,8},{6,9},{7,10},{8,11},{9,12},{10... | collective-permute-start | bytes 786440 | tf_op jit(solution)/shard_map/ppermute | solution.py:21
  15.7 23.8 %collective-permute-start.1 = (bf16[2,1,4,128,128]{4,2,3,1,0:T(4,128)(2,1)S(1)}, bf16[2,1,4,128,128]{4,2,3,1,0:T(4,128)(2,1)}, u32[]{:S(2)}, u32[]{:S(2)}) collective-permute-start(bf16[2,1,4,128,128]{4,2,3,1,0:T(4,128)(2,1)S(1)} %pad_maximum_fusion), channel_id=1, source_target_pairs={{0,2},{1,3},{2,4},{3,5},{4,6},{5,7},{6,8},{7,9},{8,10},{9,11},{10,... | collective-permute-start | bytes 786440 | tf_op jit(solution)/shard_map/ppermute | solution.py:21
  19.3 20.2 %collective-permute-start.2 = (bf16[2,1,4,128,128]{4,2,3,1,0:T(4,128)(2,1)S(1)}, bf16[2,1,4,128,128]{4,2,3,1,0:T(4,128)(2,1)}, u32[]{:S(2)}, u32[]{:S(2)}) collective-permute-start(bf16[2,1,4,128,128]{4,2,3,1,0:T(4,128)(2,1)S(1)} %pad_maximum_fusion), channel_id=1, source_target_pairs={{0,1},{1,2},{2,3},{3,4},{4,5},{5,6},{6,7},{7,8},{8,9},{9,10},{10,1... | collective-permute-start | bytes 786440 | tf_op jit(solution)/shard_map/ppermute | solution.py:21
  21.2 18.3 %collective-permute-start.3 = (bf16[2,1,4,128,128]{4,2,3,1,0:T(4,128)(2,1)S(1)}, bf16[2,1,4,128,128]{4,2,3,1,0:T(4,128)(2,1)}, u32[]{:S(2)}, u32[]{:S(2)}) collective-permute-start(bf16[2,1,4,128,128]{4,2,3,1,0:T(4,128)(2,1)S(1)} %pad_maximum_fusion), channel_id=1, source_target_pairs={{1,0},{2,1},{3,2},{4,3},{5,4},{6,5},{7,6},{8,7},{9,8},{10,9},{11,1... | collective-permute-start | bytes 786440 | tf_op jit(solution)/shard_map/ppermute | solution.py:21
  24.3 15.2 %collective-permute-start.4 = (bf16[2,1,4,128,128]{4,2,3,1,0:T(4,128)(2,1)S(1)}, bf16[2,1,4,128,128]{4,2,3,1,0:T(4,128)(2,1)}, u32[]{:S(2)}, u32[]{:S(2)}) collective-permute-start(bf16[2,1,4,128,128]{4,2,3,1,0:T(4,128)(2,1)S(1)} %pad_maximum_fusion), channel_id=1, source_target_pairs={{2,0},{3,1},{4,2},{5,3},{6,4},{7,5},{8,6},{9,7},{10,8},{11,9},{12,... | collective-permute-start | bytes 786440 | tf_op jit(solution)/shard_map/ppermute | solution.py:21
  36.2 14.1 %collective-permute-start.5 = (bf16[2,1,4,128,128]{4,2,3,1,0:T(4,128)(2,1)S(1)}, bf16[2,1,4,128,128]{4,2,3,1,0:T(4,128)(2,1)S(1)}, u32[]{:S(2)}, u32[]{:S(2)}) collective-permute-start(bf16[2,1,4,128,128]{4,2,3,1,0:T(4,128)(2,1)S(1)} %pad_maximum_fusion), channel_id=1, source_target_pairs={{3,0},{4,1},{5,2},{6,3},{7,4},{8,5},{9,6},{10,7},{11,8},{12,9},{13... | collective-permute-start | bytes 786440 | tf_op jit(solution)/shard_map/ppermute | solution.py:21
  59.7 9.0 %copy-start.1 = (bf16[9,28,128,128]{3,2,0,1:T(8,128)(2,1)}, bf16[9,28,128,128]{3,2,0,1:T(8,128)(2,1)S(1)}, u32[]{:S(2)}) copy-start(bf16[9,28,128,128]{3,2,0,1:T(8,128)(2,1)S(1)} %convert_bitcast_fusion) | copy-start | bytes 24772612
  64.2 4.4 copy-start.4
  64.2 4.4 copy-start.7
  68.6 4.6 copy-start.5
  73.3 1.9 copy-start.6
  73.9 6.1 %copy-start.9 = (pred[4,25]{1,0:T(4,128)(4,1)S(1)}, pred[4,25]{1,0:T(4,128)(4,1)}, u32[]{:S(2)}) copy-start(pred[4,25]{1,0:T(4,128)(4,1)} %iota_compare_fusion.3) | copy-start | bytes 304
  78.8 4.8 copy-start.3
  85.9 278.9 %slice-start = ((f32[1,4,128,128]{3,1,2,0:T(4,128)}), f32[1,4,126,128]{3,1,2,0:T(4,128)S(1)}, s32[]{:S(2)}) async-start(f32[1,4,128,128]{3,1,2,0:T(4,128)} %copy-done.4), calls=%async_computation.2 | async-start | bytes 516096 | tf_op jit(solution)/shard_map/jit(_roll_static)/slice | solution.py:71
  85.9 278.9 %slice-start.1 = ((f32[1,4,128,128]{3,1,2,0:T(4,128)}), f32[1,4,2,128]{3,1,2,0:T(4,128)S(1)}, s32[]{:S(2)}) async-start(f32[1,4,128,128]{3,1,2,0:T(4,128)} %copy-done.4), calls=%async_computation.3 | async-start | bytes 8192 | tf_op jit(solution)/shard_map/jit(_roll_static)/slice | solution.py:71
  86.0 278.9 %slice-start.2 = ((f32[1,4,128,128]{3,1,2,0:T(4,128)}), f32[1,4,126,128]{3,1,2,0:T(4,128)S(1)}, s32[]{:S(2)}) async-start(f32[1,4,128,128]{3,1,2,0:T(4,128)} %copy-done.5), calls=%async_computation.4 | async-start | bytes 516096 | tf_op jit(solution)/shard_map/jit(_roll_static)/slice | solution.py:71
  86.0 278.9 %slice-start.3 = ((f32[1,4,128,128]{3,1,2,0:T(4,128)}), f32[1,4,2,128]{3,1,2,0:T(4,128)S(1)}, s32[]{:S(2)}) async-start(f32[1,4,128,128]{3,1,2,0:T(4,128)} %copy-done.5), calls=%async_computation.5 | async-start | bytes 8192 | tf_op jit(solution)/shard_map/jit(_roll_static)/slice | solution.py:71
  86.0 278.9 %slice-start.4 = ((f32[1,4,128,128]{3,1,2,0:T(4,128)}), f32[1,4,127,128]{3,1,2,0:T(4,128)S(1)}, s32[]{:S(2)}) async-start(f32[1,4,128,128]{3,1,2,0:T(4,128)} %copy-done.6), calls=%async_computation.6 | async-start | bytes 520192 | tf_op jit(solution)/shard_map/jit(_roll_static)/slice | solution.py:71
  86.0 278.9 %slice-start.5 = ((f32[1,4,128,128]{3,1,2,0:T(4,128)}), f32[1,4,1,128]{3,1,2,0:T(4,128)S(1)}, s32[]{:S(2)}) async-start(f32[1,4,128,128]{3,1,2,0:T(4,128)} %copy-done.6), calls=%async_computation.7 | async-start | bytes 4096 | tf_op jit(solution)/shard_map/jit(_roll_static)/slice | solution.py:71
  86.0 478.2 %all-reduce.8.cloned.1.call-start = ((), (), s32[]{:S(2)}) async-start(), calls=%async_computation.1 | async-start | bytes 1179648 | tf_op jit(solution)/shard_map/psum | solution.py:14
Sparse Core Ops, SparseCore 0:
  86.1 278.7 all-reduce.5
  368.0 196.1 all-reduce.7
